TPU v7x, 32 devices: a whole 2x2x4 slice. The times are simulated.
32 devices in a mesh: qrow: 4 (over y, x), kcol: 4 (over z), dp: 2 (over core).
Axes of the slice: x: 2, y: 2, z: 4, core: 2. Of those that a mesh axis runs over, the one named last changes fastest.
Arguments:
- request_vectors: bfloat16 [192, 2048], P(('qrow', 'kcol'), 'dp'), may hold values from -6 to 6
- sequence_probes: bfloat16 [2048, 2048], P(('kcol', 'qrow'), 'dp'), may hold values from -6 to 6
- sequence_contents: bfloat16 [2048, 2048], P(('kcol', 'qrow'), 'dp'), may hold values from -6 to 6
- mixed_result: bfloat16 [192, 2048], P(('qrow', 'kcol'), 'dp'), may hold values from -4 to 4
- result_cotangent: bfloat16 [192, 2048], P(('qrow', 'kcol'), 'dp'), may hold values from -4 to 4
- saved_normalizer: float32 [16, 192], P('dp', ('qrow', 'kcol'))
- score_multiplier: float32 [16], P('dp'), may hold values from 0.5 to 2
- segment_spans: int32 [8], replicated, may hold values from 1 to 96, 192 in all
Outputs:
- grad_queries: bfloat16 [192, 2048], P(('qrow', 'kcol'), 'dp')
- grad_keys: bfloat16 [2048, 2048], P(('kcol', 'qrow'), 'dp')
- grad_values: bfloat16 [2048, 2048], P(('kcol', 'qrow'), 'dp')
- grad_temperature: float32 [16], replicated
Inputs may be any that keep to these rules, and one draw needn't show every extreme that they name: `segment_spans`: 8 positive document lengths summing to 192; the longest is exactly 96.
All inputs are finite; a program needn't handle non-finite values.
Results may differ from a plain program's by a relative error of at most 0.01.
Values may be sent and summed in bfloat16 or wider, within the bound.
A program may use at most 64 MiB of HBM per device.

v0:
```python
import math

import jax
import jax.numpy as jnp
from jax import lax
from jax.sharding import PartitionSpec as P


def row_delta(grad_rows, out_rows, channel_positions):
    product = grad_rows.astype(jnp.float32) * out_rows.astype(jnp.float32)
    return product.reshape(grad_rows.shape[0], channel_positions, -1).sum(axis=2).T


def shard_positions(outer_count, outer_stride, inner_index, shard):
    outer = jnp.arange(outer_count, dtype=jnp.int32)[:, None] * outer_stride + inner_index
    return (outer * shard + jnp.arange(shard, dtype=jnp.int32)[None, :]).reshape(-1)


def local(
    request_vectors,
    sequence_probes,
    sequence_contents,
    mixed_result,
    result_cotangent,
    saved_normalizer,
    score_multiplier,
    segment_spans,
):
    channel_positions = score_multiplier.shape[0]
    width = request_vectors.shape[1]
    depth = width // channel_positions
    q_shard = request_vectors.shape[0]
    k_shard = sequence_probes.shape[0]
    n_rows = lax.axis_size("qrow")
    n_cols = lax.axis_size("kcol")
    offset = (k_shard - q_shard) * n_rows * n_cols
    local_delta = row_delta(result_cotangent, mixed_result, channel_positions)
    query_block, grad_block = (
        lax.all_gather(request_vectors, "kcol", axis=0, tiled=True),
        lax.all_gather(result_cotangent, "kcol", axis=0, tiled=True),
    )
    lse_block, delta_block = (
        lax.all_gather(saved_normalizer, "kcol", axis=1, tiled=True),
        lax.all_gather(local_delta, "kcol", axis=1, tiled=True),
    )
    key_block, value_block = (
        lax.all_gather(sequence_probes, "qrow", axis=0, tiled=True),
        lax.all_gather(sequence_contents, "qrow", axis=0, tiled=True),
    )
    q_pos = offset + shard_positions(n_cols, 1, lax.axis_index("qrow") * n_cols, q_shard)
    k_pos = shard_positions(n_rows, 1, lax.axis_index("kcol") * n_rows, k_shard)
    q_count = query_block.shape[0]
    k_count = key_block.shape[0]
    starts = jnp.cumsum(segment_spans) - segment_spans + offset
    q_start = jnp.max(jnp.where(starts[None, :] <= q_pos[:, None], starts[None, :], offset), axis=1)
    allowed_mask = (k_pos[None, :] <= q_pos[:, None]) & (
        (k_pos[None, :] >= q_start[:, None]) | (k_pos[None, :] < offset)
    )
    factor_applied = 1.0 / math.sqrt(depth)
    channel_numbers = jnp.arange(channel_positions, dtype=jnp.int32)
    initial = (
        jnp.zeros((q_count, width), jnp.float32),
        jnp.zeros((k_count, width), jnp.float32),
        jnp.zeros((k_count, width), jnp.float32),
        jnp.zeros((channel_positions,), jnp.float32),
    )

    def per_head(channel_number, running_state):
        request_sensitivity, probe_sensitivity, content_sensitivity, multiplier_sensitivity = (
            running_state
        )
        start = channel_number * depth
        channel_requests = lax.dynamic_slice_in_dim(query_block, start, depth, 1)
        channel_cotangent = lax.dynamic_slice_in_dim(grad_block, start, depth, 1)
        channel_probes = lax.dynamic_slice_in_dim(key_block, start, depth, 1)
        channel_contents = lax.dynamic_slice_in_dim(value_block, start, depth, 1)
        channel_normalizer = lax.dynamic_index_in_dim(lse_block, channel_number, 0, keepdims=False)
        channel_correction = lax.dynamic_index_in_dim(
            delta_block, channel_number, 0, keepdims=False
        )
        channel_multiplier = lax.dynamic_index_in_dim(
            score_multiplier, channel_number, 0, keepdims=False
        )
        unscaled_logits = (
            jnp.einsum(
                "qd,kd->qk", channel_requests, channel_probes, preferred_element_type=jnp.float32
            )
            * factor_applied
        )
        softmax_weight = jnp.where(
            allowed_mask,
            jnp.exp(channel_multiplier * unscaled_logits - channel_normalizer[:, None]),
            0.0,
        )
        prob_b = softmax_weight.astype(jnp.bfloat16)
        dprob = jnp.einsum(
            "qd,kd->qk", channel_cotangent, channel_contents, preferred_element_type=jnp.float32
        )
        logit_cotangent = softmax_weight * (dprob - channel_correction[:, None])
        multiplier_cotangent = jnp.sum(logit_cotangent * unscaled_logits)
        probe_cotangent = (channel_multiplier * factor_applied * logit_cotangent).astype(
            jnp.bfloat16
        )
        dq_head = jnp.dot(probe_cotangent, channel_probes, preferred_element_type=jnp.float32)
        dk_head = jnp.einsum(
            "qk,qd->kd", probe_cotangent, channel_requests, preferred_element_type=jnp.float32
        )
        dv_head = jnp.einsum(
            "qk,qd->kd", prob_b, channel_cotangent, preferred_element_type=jnp.float32
        )
        request_sensitivity = lax.dynamic_update_slice_in_dim(
            request_sensitivity, dq_head, start, 1
        )
        probe_sensitivity = lax.dynamic_update_slice_in_dim(probe_sensitivity, dk_head, start, 1)
        content_sensitivity = lax.dynamic_update_slice_in_dim(
            content_sensitivity, dv_head, start, 1
        )
        multiplier_sensitivity = multiplier_sensitivity + jnp.where(
            channel_numbers == channel_number, multiplier_cotangent, 0.0
        )
        return (request_sensitivity, probe_sensitivity, content_sensitivity, multiplier_sensitivity)

    request_sensitivity, probe_sensitivity, content_sensitivity, multiplier_sensitivity = (
        lax.fori_loop(0, channel_positions, per_head, initial)
    )
    term_q = request_sensitivity.astype(jnp.bfloat16).astype(jnp.float32)
    pieces_k = probe_sensitivity.astype(jnp.bfloat16).reshape(n_rows, k_shard, width)
    pieces_v = content_sensitivity.astype(jnp.bfloat16).reshape(n_rows, k_shard, width)
    summed_q = lax.psum_scatter(
        term_q.astype(jnp.bfloat16), "kcol", scatter_dimension=0, tiled=True
    )
    landed_k, landed_v = (
        lax.all_to_all(pieces_k, "qrow", split_axis=0, concat_axis=0, tiled=True),
        lax.all_to_all(pieces_v, "qrow", split_axis=0, concat_axis=0, tiled=True),
    )
    summed_k = jnp.sum(landed_k.astype(jnp.float32), axis=0)
    summed_v = jnp.sum(landed_v.astype(jnp.float32), axis=0)
    every_channel = jnp.zeros((channel_positions * lax.axis_size("dp"),), jnp.float32)
    every_channel = lax.dynamic_update_slice_in_dim(
        every_channel, multiplier_sensitivity, lax.axis_index("dp") * channel_positions, 0
    )
    total_tau = lax.psum(every_channel, ("qrow", "kcol", "dp"))
    return (summed_q, summed_k.astype(jnp.bfloat16), summed_v.astype(jnp.bfloat16), total_tau)


def solution(mesh):
    in_specs = (
        P(("qrow", "kcol"), "dp"),
        P(("kcol", "qrow"), "dp"),
        P(("kcol", "qrow"), "dp"),
        P(("qrow", "kcol"), "dp"),
        P(("qrow", "kcol"), "dp"),
        P("dp", ("qrow", "kcol")),
        P("dp"),
        P(),
    )
    out_specs = (
        P(("qrow", "kcol"), "dp"),
        P(("kcol", "qrow"), "dp"),
        P(("kcol", "qrow"), "dp"),
        P(),
    )
    return jax.shard_map(local, mesh=mesh, in_specs=in_specs, out_specs=out_specs, check_vma=False)
```

profile of v0, /device:TPU:0, one launch (start us, length us, event | category | flops | bytes accessed | tf_op | source)
XLA Modules:
  0.0 212.9 jit_solution(6358460647126907544)
XLA Ops:
  8.0 0.7 all-gather.9.cloned.1.call-update
  9.4 15.0 %all-gather = bf16[4,12,1024]{2,1,0:T(8,128)(2,1)S(1)} all-gather(bf16[1,12,1024]{2,1,0:T(8,128)(2,1)S(1)} %bitcast.42), channel_id=1, replica_groups=mesh['qrow'=4,'kcol'=4,'dp'=2] {'kcol'}, dimensions={0}, use_global_device_ids=true | all-gather | bytes 122880 | tf_op jit(solution)/shard_map/all_gather | solution.py:39
  24.5 0.7 copy-done
  25.2 13.6 %all-gather.2 = bf16[4,12,1024]{2,1,0:T(8,128)(2,1)S(1)} all-gather(bf16[1,12,1024]{2,1,0:T(8,128)(2,1)S(1)} %bitcast.41), channel_id=1, replica_groups=mesh['qrow'=4,'kcol'=4,'dp'=2] {'kcol'}, dimensions={0}, use_global_device_ids=true | all-gather | bytes 122880 | tf_op jit(solution)/shard_map/all_gather | solution.py:40
  38.9 0.7 copy-done.2
  39.8 13.1 %all-gather.3 = f32[4,12,8]{1,2,0:T(8,128)S(1)} all-gather(f32[1,12,8]{1,2,0:T(8,128)S(1)} %bitcast.43), channel_id=1, replica_groups=mesh['qrow'=4,'kcol'=4,'dp'=2] {'kcol'}, dimensions={0}, use_global_device_ids=true | all-gather | bytes 1920 | tf_op jit(solution)/shard_map/all_gather | solution.py:44
  53.6 13.1 %all-gather.1 = f32[4,12,8]{1,2,0:T(8,128)S(1)} all-gather(f32[1,12,8]{1,2,0:T(8,128)S(1)} %bitcast.46), channel_id=1, replica_groups=mesh['qrow'=4,'kcol'=4,'dp'=2] {'kcol'}, dimensions={0}, use_global_device_ids=true | all-gather | bytes 1920 | tf_op jit(solution)/shard_map/all_gather | solution.py:43
  67.8 1.1 broadcast.69.clone
  69.6 55.9 %while.20 = (s32[]{:T(128)}, bf16[48,1024]{1,0:T(8,128)(2,1)S(1)}, bf16[512,1024]{1,0:T(8,128)(2,1)S(1)}, bf16[512,1024]{1,0:T(8,128)(2,1)}, f32[8]{0:T(128)S(1)...) while((s32[]{:T(128)}, bf16[48,1024]{1,0:T(8,128)(2,1)S(1)}, ...), condition=%wide.region_5.6_spmd.clone, body=%wide.region_3.5_spmd.clone.sunk | while | flops 32047140 | bytes 1597537 | solution.py:124
  69.6 1.1 fusion.48
  71.9 1.7 multiply_reduce_fusion.2
  73.9 1.0 convolution_dynamic-update-slice_fusion.8
  74.8 1.1 convolution_dynamic-update-slice_fusion.6
  76.6 1.1 fusion.48
  78.9 1.7 multiply_reduce_fusion.2
  80.8 1.0 convolution_dynamic-update-slice_fusion.8
  81.8 1.1 convolution_dynamic-update-slice_fusion.6
  83.6 1.1 fusion.48
  85.9 1.7 multiply_reduce_fusion.2
  87.8 1.0 convolution_dynamic-update-slice_fusion.8
  88.8 1.1 convolution_dynamic-update-slice_fusion.6
  90.5 1.1 fusion.48
  92.9 1.7 multiply_reduce_fusion.2
  94.8 1.0 convolution_dynamic-update-slice_fusion.8
  95.8 1.1 convolution_dynamic-update-slice_fusion.6
  97.5 1.1 fusion.48
  99.8 1.7 multiply_reduce_fusion.2
  101.8 1.0 convolution_dynamic-update-slice_fusion.8
  102.8 1.1 convolution_dynamic-update-slice_fusion.6
  104.5 1.1 fusion.48
  106.8 1.7 multiply_reduce_fusion.2
  108.8 1.0 convolution_dynamic-update-slice_fusion.8
  109.7 1.1 convolution_dynamic-update-slice_fusion.6
  111.5 1.1 fusion.48
  113.8 1.7 multiply_reduce_fusion.2
  115.7 1.0 convolution_dynamic-update-slice_fusion.8
  116.7 1.1 convolution_dynamic-update-slice_fusion.6
  118.5 1.1 fusion.48
  120.8 1.7 multiply_reduce_fusion.2
  122.7 1.0 convolution_dynamic-update-slice_fusion.8
  123.7 1.1 convolution_dynamic-update-slice_fusion.6
  125.5 16.8 %all_to_all.10 = bf16[4,128,1024]{2,1,0:T(8,128)(2,1)S(1)} all-to-all(bf16[4,128,1024]{2,1,0:T(8,128)(2,1)S(1)} %bitcast.38), channel_id=1, replica_groups=mesh['qrow'=4,'kcol'=4,'dp'=2] {'qrow'}, dimensions={0} | all-to-all | bytes 2097152 | tf_op jit(solution)/shard_map/all_to_all | solution.py:133
  142.3 3.5 %all-to-all-start.1 = ((bf16[4,128,1024]{2,1,0:T(8,128)(2,1)}), bf16[4,128,1024]{2,1,0:T(8,128)(2,1)S(1)}, u32[]{:S(2)}, u32[]{:S(2)}) async-start(bf16[4,128,1024]{2,1,0:T(8,128)(2,1)} %bitcast.11), calls=%async_computation.1 | async-start | bytes 2097152 | tf_op jit(solution)/shard_map/all_to_all | solution.py:134
  145.8 13.5 %fusion.4 = bf16[16,1024]{1,0:T(8,128)(2,1)S(1)} fusion(bf16[48,1024]{1,0:T(8,128)(2,1)S(1)} %get-tuple-element.236), kind=kCustom, calls=%all-reduce-scatter | all-reduce-scatter fusion | flops 65537 | bytes 131584
  159.3 2.7 %collective-permute-start = (bf16[12,1024]{1,0:T(8,128)(2,1)S(1)}, bf16[12,1024]{1,0:T(8,128)(2,1)S(1)}, u32[]{:S(2)}, u32[]{:S(2)}) collective-permute-start(bf16[12,1024]{1,0:T(8,128)(2,1)S(1)} %slice), channel_id=1, source_target_pairs={{0,2},{2,4},{4,6},{1,3},{3,5},{5,7},{8,10},{10,12},{12,14},{9,11},... | collective-permute-start | bytes 73736
  164.1 39.2 %psum.7 = f32[16]{0:T(128)} all-reduce(f32[16]{0:T(128)S(1)} %dynamic_update_slice.24), channel_id=1, replica_groups=mesh['qrow'=4,'kcol'=4,'dp'=2] {'qrow','kcol','dp'}, use_global_device_ids=true, to_apply=%region_9.10 | all-reduce | flops 16 | bytes 128 | tf_op jit(solution)/shard_map/psum | solution.py:142
  204.2 0.9 reduce_sum.47
  205.1 0.9 reduce_sum.48
  (79 shorter events, 18.3 us)
Async XLA Ops:
  7.2 59.9 %all-gather.7.cloned.1.call-start = ((), (), s32[]{:S(2)}) async-start(), calls=%async_computation.2 | async-start | bytes 1310720 | tf_op jit(solution)/shard_map/all_gather | solution.py:47
  7.9 59.8 %all-gather.9.cloned.1.call-start = ((), (), s32[]{:S(2)}) async-start(), calls=%async_computation.3 | async-start | bytes 1310720 | tf_op jit(solution)/shard_map/all_gather | solution.py:48
  7.9 0.9 copy-start.5
  8.6 0.8 copy-start.1
  24.5 0.8 copy-start
  38.8 0.8 copy-start.2
  52.9 0.7 copy-start.3
  68.9 0.7 copy-start.6
  142.3 62.8 %all-to-all-start.1 = ((bf16[4,128,1024]{2,1,0:T(8,128)(2,1)}), bf16[4,128,1024]{2,1,0:T(8,128)(2,1)S(1)}, u32[]{:S(2)}, u32[]{:S(2)}) async-start(bf16[4,128,1024]{2,1,0:T(8,128)(2,1)} %bitcast.11), calls=%async_computation.1 | async-start | bytes 2097152 | tf_op jit(solution)/shard_map/all_to_all | solution.py:134
  159.3 44.0 %collective-permute-start = (bf16[12,1024]{1,0:T(8,128)(2,1)S(1)}, bf16[12,1024]{1,0:T(8,128)(2,1)S(1)}, u32[]{:S(2)}, u32[]{:S(2)}) collective-permute-start(bf16[12,1024]{1,0:T(8,128)(2,1)S(1)} %slice), channel_id=1, source_target_pairs={{0,2},{2,4},{4,6},{1,3},{3,5},{5,7},{8,10},{10,12},{12,14},{9,11},... | collective-permute-start | bytes 73736
  162.0 0.7 copy-start.4
Sparse Core Ops, SparseCore 0:
  9.8 29.3 all-gather.6
  41.0 26.6 all-gather.8
where the time goes:
time: 214 us; the launch traced here: 213 us
  blocking collectives  124 us (58%)
  matrix products  40.2 us (19%)
  between operations  14.8 us (7%)
  local copies, waits for them, and re-layouts  11.8 us (6%)
  other arithmetic  7.72 us (4%)
  starting transfers between devices  6.26 us (3%)
  loops' own time  5.63 us (3%)
    psum x1, blocking collectives, local(): total_tau = lax.psum(every_channel, ('qrow', 'kcol', 'dp'))  39.2 us
    all_to_all x1, blocking collectives, local(): lax.all_to_all(pieces_k, 'qrow', split_axis=0, concat_axis=0, tiled=True)  16.8 us
    all_gather x1, blocking collectives, local(): lax.all_gather(request_vectors, 'kcol', axis=0, tiled=True)  15 us
    all_gather x1, blocking collectives, local(): lax.all_gather(result_cotangent, 'kcol', axis=0, tiled=True)  13.6 us
    dot_general x8, matrix products, per_head(): jnp.einsum('qd,kd->qk', channel_cotangent, channel_contents, preferred_el...  13.6 us
    unnamed x1, blocking collectives  13.5 us
    all_gather x1, blocking collectives, local(): lax.all_gather(local_delta, 'kcol', axis=1, tiled=True)  13.1 us
    all_gather x1, blocking collectives, local(): lax.all_gather(saved_normalizer, 'kcol', axis=1, tiled=True)  13.1 us
  transfers between devices with their start and end apart: 4, of which 1 were waited for; matrix products, arithmetic and copies ran while one was open for 8% of the time, Pallas kernels for 0%

commit v1 on v0

v1 whole, which is shorter than its diff:
```python
import functools
import math

import jax
import jax.numpy as jnp
from jax import lax
from jax.experimental import pallas as pl
from jax.experimental.pallas import tpu as pltpu
from jax.sharding import PartitionSpec as P

MESH = pl.DeviceIdType.MESH
F32 = jnp.float32
BF16 = jnp.bfloat16


def kernel(
    dims,
    q_ref, k_ref, v_ref, o_ref, g_ref, lse_ref, mult_ref, spans_ref,
    dq_ref, dk_ref, dv_ref, tau_ref,
    pack32, asm32, gath, stat1, blk, stat, prob_s, grad_s, dqs, dqr, dq0, dqz, tau_acc, tau_a, tau_b,
    s1, r1, s1s, r1s, s2, r2, s2s, r2s, sa, ra, sb, rb, sta, rta, stb, rtb,
):
    n_rows, n_cols, n_dp, heads, depth, qs, ks, lanes = dims
    rows = n_cols * qs
    hq = heads * qs
    qrow = lax.axis_index("qrow")
    kcol = lax.axis_index("kcol")
    dp = lax.axis_index("dp")
    flat = dp * n_rows + qrow
    n_flat = n_dp * n_rows
    offset = (ks - qs) * n_rows * n_cols
    factor = 1.0 / math.sqrt(depth)

    barrier = pltpu.get_barrier_semaphore()

    @pl.loop(1, n_cols)
    def _(j):
        pl.semaphore_signal(
            barrier, inc=1, device_id={"kcol": lax.rem(kcol + j, n_cols)}, device_id_type=MESH
        )

    @pl.loop(1, n_flat)
    def _(t):
        peer = lax.rem(flat + t, n_flat)
        pl.semaphore_signal(
            barrier,
            inc=1,
            device_id={"qrow": lax.rem(peer, n_rows), "dp": peer // n_rows},
            device_id_type=MESH,
        )

    q32 = q_ref[...].astype(F32)
    g32 = g_ref[...].astype(F32)
    prod = g32 * o_ref[...].astype(F32)
    lane = lax.broadcasted_iota(jnp.int32, (qs, 128), 1)
    delta = jnp.zeros((qs, 128), F32)
    for h in range(heads):
        cols = slice(h * depth, (h + 1) * depth)
        pack32[h * qs : (h + 1) * qs, :] = q32[:, cols]
        pack32[hq + h * qs : hq + (h + 1) * qs, :] = g32[:, cols]
        delta = jnp.where(lane == h, jnp.sum(prod[:, cols], axis=1, keepdims=True), delta)
    gath[kcol] = pack32[...].astype(BF16)
    asm32[0:128, :] = jnp.zeros((128, 128), F32)
    asm32[0:qs, :] = delta
    delta_t = asm32[0:128, :].T
    asm32[0:heads, :] = jnp.zeros((heads, 128), F32)
    asm32[0:heads, 0:qs] = lse_ref[...]
    both = jnp.concatenate([asm32[0:heads, :], delta_t[0:heads, :]], axis=0)
    if lanes > 128:
        both = jnp.concatenate([both, jnp.zeros((2 * heads, lanes - 128), F32)], axis=1)
    stat1[kcol] = pltpu.roll(both, kcol * qs, 1)
    tau_acc[...] = jnp.zeros_like(tau_acc)

    pl.semaphore_wait(barrier, n_cols - 1 + n_flat - 1)

    def gather_copy(j, which):
        peer = {"kcol": lax.rem(kcol + j, n_cols)}
        buf, ss, rs = which
        return pltpu.make_async_remote_copy(
            src_ref=buf.at[kcol], dst_ref=buf.at[kcol],
            send_sem=ss.at[j], recv_sem=rs.at[j], device_id=peer, device_id_type=MESH,
        )

    first = ((gath, s1, r1), (stat1, s1s, r1s))

    @pl.loop(1, n_cols)
    def _(j):
        for which in first:
            gather_copy(j, which).start()

    def gather_wait(j):
        source = lax.rem(kcol - j + n_cols, n_cols)
        for buf, ss, rs in first:
            pltpu.make_async_remote_copy(
                src_ref=buf.at[source], dst_ref=buf.at[source],
                send_sem=ss.at[j], recv_sem=rs.at[j],
                device_id={"kcol": lax.rem(kcol + j, n_cols)}, device_id_type=MESH,
            ).wait_recv()

    @pl.loop(1, n_cols)
    def _(j):
        gather_wait(j)

    total = stat1[0]
    for z in range(1, n_cols):
        total = total + stat1[z]
    stat[0] = total
    for z in range(n_cols):
        pack32[...] = gath[z].astype(F32)
        for h in range(2 * heads):
            asm32[h * rows + z * qs : h * rows + (z + 1) * qs, :] = pack32[h * qs : (h + 1) * qs, :]
    blk[0] = asm32[...].astype(BF16)

    second = ((blk, s2, r2), (stat, s2s, r2s))

    def exchange_copy(i, which):
        buf, ss, rs = which
        return pltpu.make_async_remote_copy(
            src_ref=buf.at[0], dst_ref=buf.at[i],
            send_sem=ss.at[i], recv_sem=rs.at[i],
            device_id={"qrow": lax.rem(qrow + i, n_rows)}, device_id_type=MESH,
        )

    def term_copy(i):
        return pltpu.make_async_remote_copy(
            src_ref=dqs.at[i], dst_ref=dqr.at[i],
            send_sem=sa.at[i], recv_sem=ra.at[i],
            device_id={"qrow": lax.rem(qrow - i + n_rows, n_rows)}, device_id_type=MESH,
        )

    @pl.loop(1, n_rows)
    def _(i):
        for which in second:
            exchange_copy(i, which).start()

    k_pos = (kcol * n_rows + qrow) * ks + lax.broadcasted_iota(jnp.int32, (rows, ks), 1)

    def tile(i, own):
        group = lax.rem(qrow - i + n_rows, n_rows)
        columns = jnp.concatenate(
            [stat[i], jnp.zeros((128 - 2 * heads, lanes), F32)], axis=0
        ).T
        q_pos = offset + rows * group + lax.broadcasted_iota(jnp.int32, (rows, ks), 0)
        start = jnp.full((rows, ks), offset, jnp.int32)
        begin = offset
        for d in range(spans_ref.shape[0]):
            start = jnp.where(begin <= q_pos, begin, start)
            begin = begin + spans_ref[d]
        mask = (k_pos <= q_pos) & ((k_pos >= start) | (k_pos < offset))
        at = pl.ds(pl.multiple_of(i * rows, 16), rows)
        for h in range(heads):
            cols = slice(h * depth, (h + 1) * depth)
            q = blk[i, h * rows : (h + 1) * rows, :]
            g = blk[i, (heads + h) * rows : (heads + h + 1) * rows, :]
            k = k_ref[:, cols]
            v = v_ref[:, cols]
            mult = mult_ref[h]
            nt = (((1,), (1,)), ((), ()))
            raw = lax.dot_general(q, k, nt, preferred_element_type=F32) * factor
            dprob = lax.dot_general(g, v, nt, preferred_element_type=F32)
            prob = jnp.where(mask, jnp.exp(mult * raw - columns[0:rows, h : h + 1]), 0.0)
            ds = prob * (dprob - columns[0:rows, heads + h : heads + h + 1])
            tau_acc[h] += jnp.sum((ds * raw).reshape(rows // 8, 8, ks), axis=0)
            gb = ((mult * factor) * ds).astype(BF16)
            prob_s[h, at, :] = prob.astype(BF16)
            grad_s[h, at, :] = gb
            term = jnp.dot(gb, k, preferred_element_type=F32)
            if own:
                dq0[h * rows : (h + 1) * rows, :] = term
            else:
                dqs[i, h * rows : (h + 1) * rows, :] = term.astype(BF16)

    tile(0, True)

    @pl.loop(1, n_rows)
    def _(i):
        for which in second:
            exchange_copy(i, which).wait_recv()
        tile(i, False)
        term_copy(i).start()

    tau_a[flat] = jnp.sum(tau_acc[...], axis=1)

    def tau_copy(t):
        peer = lax.rem(flat + t, n_flat)
        return pltpu.make_async_remote_copy(
            src_ref=tau_a.at[flat], dst_ref=tau_a.at[flat],
            send_sem=sta.at[t], recv_sem=rta.at[t],
            device_id={"qrow": lax.rem(peer, n_rows), "dp": peer // n_rows}, device_id_type=MESH,
        )

    def tau_wait(t):
        peer = lax.rem(flat + t, n_flat)
        source = lax.rem(flat - t + n_flat, n_flat)
        pltpu.make_async_remote_copy(
            src_ref=tau_a.at[source], dst_ref=tau_a.at[source],
            send_sem=sta.at[t], recv_sem=rta.at[t],
            device_id={"qrow": lax.rem(peer, n_rows), "dp": peer // n_rows}, device_id_type=MESH,
        ).wait_recv()

    @pl.loop(1, n_flat)
    def _(t):
        tau_copy(t).start()

    tn = (((0,), (0,)), ((), ()))

    def keys(h):
        cols = slice(h * depth, (h + 1) * depth)
        q_all = blk[:, h * rows : (h + 1) * rows, :].reshape(n_rows * rows, depth)
        g_all = blk[:, (heads + h) * rows : (heads + h + 1) * rows, :].reshape(n_rows * rows, depth)
        dk_ref[:, cols] = lax.dot_general(
            grad_s[h], q_all, tn, preferred_element_type=F32
        ).astype(BF16)
        dv_ref[:, cols] = lax.dot_general(
            prob_s[h], g_all, tn, preferred_element_type=F32
        ).astype(BF16)

    for h in range(heads // 2):
        keys(h)

    @pl.loop(1, n_rows)
    def _(i):
        term_copy(i).wait_recv()
        dq0[...] += dqr[i].astype(F32)

    for z in range(n_cols):
        for h in range(heads):
            pack32[h * qs : (h + 1) * qs, :] = dq0[h * rows + z * qs : h * rows + (z + 1) * qs, :]
        dqz[0, z] = pack32[0:hq, :].astype(BF16)

    @pl.loop(1, n_flat)
    def _(t):
        tau_wait(t)

    tau_b[kcol] = jnp.sum(
        tau_a[...].reshape(n_dp, n_rows, heads, 128), axis=1
    ).reshape(n_dp * heads, 128)

    def last_copy(j):
        z = lax.rem(kcol + j, n_cols)
        return pltpu.make_async_remote_copy(
            src_ref=dqz.at[0, z], dst_ref=dqz.at[1, j],
            send_sem=sb.at[j], recv_sem=rb.at[j], device_id={"kcol": z}, device_id_type=MESH,
        )

    def last_tau(j):
        return pltpu.make_async_remote_copy(
            src_ref=tau_b.at[kcol], dst_ref=tau_b.at[kcol],
            send_sem=stb.at[j], recv_sem=rtb.at[j],
            device_id={"kcol": lax.rem(kcol + j, n_cols)}, device_id_type=MESH,
        )

    def last_tau_wait(j):
        source = lax.rem(kcol - j + n_cols, n_cols)
        pltpu.make_async_remote_copy(
            src_ref=tau_b.at[source], dst_ref=tau_b.at[source],
            send_sem=stb.at[j], recv_sem=rtb.at[j],
            device_id={"kcol": lax.rem(kcol + j, n_cols)}, device_id_type=MESH,
        ).wait_recv()

    @pl.loop(1, n_cols)
    def _(j):
        last_copy(j).start()
        last_tau(j).start()

    for h in range(heads // 2, heads):
        keys(h)

    pack32[0:hq, :] = dqz[0, kcol].astype(F32)

    @pl.loop(1, n_cols)
    def _(j):
        last_copy(j).wait_recv()
        pack32[0:hq, :] += dqz[1, j].astype(F32)

    for h in range(heads):
        dq_ref[:, h * depth : (h + 1) * depth] = pack32[h * qs : (h + 1) * qs, :].astype(BF16)

    @pl.loop(1, n_cols)
    def _(j):
        last_tau_wait(j)

    tau = jnp.sum(tau_b[...], axis=0)
    tau = jnp.concatenate([tau, jnp.zeros((128 - n_dp * heads, 128), F32)], axis=0).T
    tau_ref[...] = jnp.sum(tau, axis=0, keepdims=True)[:, 0 : n_dp * heads]

    @pl.loop(1, n_cols)
    def _(j):
        for which in first:
            gather_copy(j, which).wait_send()
        last_copy(j).wait_send()
        last_tau(j).wait_send()

    @pl.loop(1, n_rows)
    def _(i):
        for which in second:
            exchange_copy(i, which).wait_send()
        term_copy(i).wait_send()

    @pl.loop(1, n_flat)
    def _(t):
        tau_copy(t).wait_send()


def local(q, k, v, o, g, lse, mult, spans):
    heads = mult.shape[0]
    qs, width = q.shape
    ks = k.shape[0]
    depth = width // heads
    n_rows = lax.axis_size("qrow")
    n_cols = lax.axis_size("kcol")
    n_dp = lax.axis_size("dp")
    rows = n_cols * qs
    lanes = -(-rows // 128) * 128
    dims = (n_rows, n_cols, n_dp, heads, depth, qs, ks, lanes)
    n_flat = n_rows * n_dp
    vmem = pl.BlockSpec(memory_space=pltpu.VMEM)
    smem = pl.BlockSpec(memory_space=pltpu.SMEM)
    dma = pltpu.SemaphoreType.DMA
    macs = 5 * heads * n_rows * rows * ks * depth
    dq, dk, dv, tau = pl.pallas_call(
        functools.partial(kernel, dims),
        out_shape=(
            jax.ShapeDtypeStruct((qs, width), BF16),
            jax.ShapeDtypeStruct((ks, width), BF16),
            jax.ShapeDtypeStruct((ks, width), BF16),
            jax.ShapeDtypeStruct((1, n_dp * heads), F32),
        ),
        in_specs=[vmem] * 6 + [smem] * 2,
        out_specs=(vmem,) * 4,
        scratch_shapes=[
            pltpu.VMEM((2 * heads * qs, depth), F32),
            pltpu.VMEM((2 * heads * rows, depth), F32),
            pltpu.VMEM((n_cols, 2 * heads * qs, depth), BF16),
            pltpu.VMEM((n_cols, 2 * heads, lanes), F32),
            pltpu.VMEM((n_rows, 2 * heads * rows, depth), BF16),
            pltpu.VMEM((n_rows, 2 * heads, lanes), F32),
            pltpu.VMEM((heads, n_rows * rows, ks), BF16),
            pltpu.VMEM((heads, n_rows * rows, ks), BF16),
            pltpu.VMEM((n_rows, heads * rows, depth), BF16),
            pltpu.VMEM((n_rows, heads * rows, depth), BF16),
            pltpu.VMEM((heads * rows, depth), F32),
            pltpu.VMEM((2, n_cols, heads * qs, depth), BF16),
            pltpu.VMEM((heads, 8, ks), F32),
            pltpu.VMEM((n_flat, heads, 128), F32),
            pltpu.VMEM((n_cols, n_dp * heads, 128), F32),
            dma((n_cols,)), dma((n_cols,)), dma((n_cols,)), dma((n_cols,)),
            dma((n_rows,)), dma((n_rows,)), dma((n_rows,)), dma((n_rows,)),
            dma((n_rows,)), dma((n_rows,)), dma((n_cols,)), dma((n_cols,)),
            dma((n_flat,)), dma((n_flat,)), dma((n_cols,)), dma((n_cols,)),
        ],
        compiler_params=pltpu.CompilerParams(
            collective_id=0, has_side_effects=True, vmem_limit_bytes=56 * 1024 * 1024
        ),
        cost_estimate=pl.CostEstimate(
            flops=2 * macs, bytes_accessed=8 * ks * width, transcendentals=heads * n_rows * rows * ks
        ),
    )(q, k, v, o, g, lse, mult, spans)
    return dq, dk, dv, tau.reshape(-1)


def solution(mesh):
    in_specs = (
        P(("qrow", "kcol"), "dp"),
        P(("kcol", "qrow"), "dp"),
        P(("kcol", "qrow"), "dp"),
        P(("qrow", "kcol"), "dp"),
        P(("qrow", "kcol"), "dp"),
        P("dp", ("qrow", "kcol")),
        P("dp"),
        P(),
    )
    out_specs = (
        P(("qrow", "kcol"), "dp"),
        P(("kcol", "qrow"), "dp"),
        P(("kcol", "qrow"), "dp"),
        P(),
    )
    return jax.shard_map(local, mesh=mesh, in_specs=in_specs, out_specs=out_specs, check_vma=False)
```

time: 214 us -> 42 us (0.20)
  blocking collectives: 124 us -> 0 us
  matrix products: 40.2 us -> 0 us
  Pallas kernels: 0 us -> 36.8 us
  between operations: 14.8 us -> 0.65 us
  other arithmetic: 7.72 us -> 0 us
  local copies, waits for them, and re-layouts: 11.8 us -> 4.31 us
  starting transfers between devices: 6.26 us -> 0 us
  loops' own time: 5.63 us -> 0 us
    all_gather x4 -> x0, blocking collectives: 54.9 us -> none  [the longest x1 15 us: local(): lax.all_gather(request_vectors, 'kcol', axis=0, tiled=True)]
    dot_general x40 -> x0, matrix products: 40.2 us -> none  [the longest x8 13.6 us: per_head(): jnp.einsum('qd,kd->qk', channel_cotangent, channel_contents, preferred_el...]
    psum x1 -> x0, blocking collectives: 39.2 us -> none  [local(): total_tau = lax.psum(every_channel, ('qrow', 'kcol', 'dp'))]
    pallas_call x0 -> x1, Pallas kernels: none -> 36.8 us  [local(): pl.pallas_call(functools.partial(kernel, dims), out_shape=(jax.ShapeDtype...]
    all_to_all x1 -> x0, blocking collectives: 16.8 us -> none  [local(): lax.all_to_all(pieces_k, 'qrow', split_axis=0, concat_axis=0, tiled=True)]
    unnamed x1 -> x0, blocking collectives: 13.5 us -> none
    another operation x1 -> x0, loops' own time: 5.63 us -> none  [local(): lax.fori_loop(0, channel_positions, per_head, initial)]
    add x11 -> x0, other arithmetic: 5.41 us -> none  [the longest x8 5.27 us: per_head(): multiplier_sensitivity + jnp.where(channel_numbers == channel_number, mul...]
  transfers between devices with their start and end apart: 4 -> 0, of which waited for: 1 -> 0; matrix products, arithmetic and copies ran while one was open for 8% -> 0% of each run, Pallas kernels for 0% -> 0%
where the time goes in v1:
time: 42 us; the launch traced here: 41.7 us
  Pallas kernels  36.8 us (88%)
  local copies, waits for them, and re-layouts  4.31 us (10%)
  between operations  0.65 us (2%)
    pallas_call x1, Pallas kernels, local(): pl.pallas_call(functools.partial(kernel, dims), out_shape=(jax.ShapeDtype...  36.8 us
    unnamed x8, local copies, waits for them, and re-layouts  4.31 us

profile of v1, /device:TPU:0, one launch (start us, length us, event | category | flops | bytes accessed | tf_op | source)
XLA Modules:
  0.0 41.7 jit_solution(16703899777919579875)
XLA Ops:
  0.6 36.8 %shard_map.111 = (bf16[12,1024]{1,0:T(8,128)(2,1)}, bf16[128,1024]{1,0:T(8,128)(2,1)}, bf16[128,1024]{1,0:T(8,128)(2,1)}, f32[1,16]{1,0:T(1,128)}) custom-call(bf16[12,1024]{1,0:T(8,128)(2,1)} %q_ref.1, bf16[128,1024]{1,0:T(8,128)(2,1)} %k_ref.1, bf16[128,1024]{1,0:T(8,128)(2,1)} %v_ref.1, bf16[12,1024]{1,0:T(8,128)(2,1)} %o_ref.1, bf16[12,1024]{1,0:T(8,128)(2,1)} %g_ref.1, ...), custom_call_target="tpu_custom_call" | custom-call | flops 251658240 | bytes 1048576 | tf_op jit(solution)/shard_map/pallas_call | solution.py:321
  37.4 1.4 %copy.16 = bf16[12,1024]{1,0:T(8,128)(2,1)} copy(bf16[12,1024]{1,0:T(8,128)(2,1)} %get-tuple-element.16) | data formatting | bytes 49152
  38.8 0.0 copy-start
  38.8 1.7 %copy.17 = bf16[128,1024]{1,0:T(8,128)(2,1)} copy(bf16[128,1024]{1,0:T(8,128)(2,1)} %get-tuple-element.17) | data formatting | bytes 524288
  40.5 0.0 copy-done
  40.5 0.0 copy-start.1
  40.5 0.7 %copy.18 = bf16[128,1024]{1,0:T(8,128)(2,1)} copy(bf16[128,1024]{1,0:T(8,128)(2,1)S(1)} %copy-done) | data formatting | bytes 524288
  41.2 0.0 copy-done.1
  41.2 0.5 %copy.19 = f32[16]{0:T(128)} copy(f32[16]{0:T(128)S(1)} %bitcast.1) | data formatting | bytes 128
Async XLA Ops:
  38.8 1.7 %copy-start = (bf16[128,1024]{1,0:T(8,128)(2,1)S(1)}, bf16[128,1024]{1,0:T(8,128)(2,1)}, u32[]{:S(2)}) copy-start(bf16[128,1024]{1,0:T(8,128)(2,1)} %get-tuple-element.18) | copy-start | bytes 786436
  40.5 0.7 %copy-start.1 = (f32[1,16]{1,0:T(1,128)S(1)}, f32[1,16]{1,0:T(1,128)}, u32[]{:S(2)}) copy-start(f32[1,16]{1,0:T(1,128)} %get-tuple-element.11) | copy-start | bytes 196

commit v2 on v1

v2 whole, which is shorter than its diff:
```python
import functools
import math

import jax
import jax.numpy as jnp
from jax import lax
from jax.experimental import pallas as pl
from jax.experimental.pallas import tpu as pltpu
from jax.sharding import PartitionSpec as P

MESH = pl.DeviceIdType.MESH
F32 = jnp.float32
BF16 = jnp.bfloat16


CHUNKS = 2


def kernel(
    dims,
    q_ref, k_hbm, v_hbm, o_ref, g_ref, lse_ref, mult_ref, spans_ref,
    dq_ref, dk_hbm, dv_hbm, tau_ref,
    k_ref, v_ref, dk_ref, dv_ref, pack32, asm32, gath, stat1, blk, stat, cols_s, mask_s,
    prob_s, grad_s, dqs, dqr, dq0, dqz, tau_acc, tau_a, tau_b,
    local_sem, s1, r1, s1s, r1s, s2, r2, s2s, r2s, sa, ra, sb, rb, sta, rta, stb, rtb,
):
    n_rows, n_cols, n_dp, heads, depth, qs, ks, lanes, chunks = dims
    hc = heads // chunks
    rows = n_cols * qs
    half = hc * qs
    qrow = lax.axis_index("qrow")
    kcol = lax.axis_index("kcol")
    dp = lax.axis_index("dp")
    flat = dp * n_rows + qrow
    n_flat = n_dp * n_rows
    offset = (ks - qs) * n_rows * n_cols
    factor = 1.0 / math.sqrt(depth)

    barrier = pltpu.get_barrier_semaphore()

    @pl.loop(1, n_cols)
    def _(j):
        pl.semaphore_signal(
            barrier, inc=1, device_id={"kcol": lax.rem(kcol + j, n_cols)}, device_id_type=MESH
        )

    @pl.loop(1, n_flat)
    def _(t):
        peer = lax.rem(flat + t, n_flat)
        pl.semaphore_signal(
            barrier,
            inc=1,
            device_id={"qrow": lax.rem(peer, n_rows), "dp": peer // n_rows},
            device_id_type=MESH,
        )

    load_k = pltpu.make_async_copy(k_hbm, k_ref, local_sem.at[0])
    load_v = pltpu.make_async_copy(v_hbm, v_ref, local_sem.at[1])
    load_k.start()
    load_v.start()

    q32 = q_ref[...].astype(F32)
    g32 = g_ref[...].astype(F32)
    for c in range(chunks):
        for e in range(hc):
            h = c * hc + e
            cols = slice(h * depth, (h + 1) * depth)
            pack32[e * qs : (e + 1) * qs, :] = q32[:, cols]
            pack32[half + e * qs : half + (e + 1) * qs, :] = g32[:, cols]
        gath[c, kcol] = pack32[...].astype(BF16)
    prod = g32 * o_ref[...].astype(F32)
    lane = lax.broadcasted_iota(jnp.int32, (qs, 128), 1)
    delta = jnp.zeros((qs, 128), F32)
    for h in range(heads):
        part = jnp.sum(prod[:, h * depth : (h + 1) * depth], axis=1, keepdims=True)
        delta = jnp.where(lane == h, part, delta)
    asm32[0:128, :] = jnp.zeros((128, 128), F32)
    asm32[0:qs, :] = delta
    delta_t = asm32[0:128, :].T
    asm32[0:heads, :] = jnp.zeros((heads, 128), F32)
    asm32[0:heads, 0:qs] = lse_ref[...]
    both = jnp.concatenate([asm32[0:heads, :], delta_t[0:heads, :]], axis=0)
    if lanes > 128:
        both = jnp.concatenate([both, jnp.zeros((2 * heads, lanes - 128), F32)], axis=1)
    stat1[kcol] = pltpu.roll(both, kcol * qs, 1)
    tau_acc[...] = jnp.zeros_like(tau_acc)

    pl.semaphore_wait(barrier, n_cols - 1 + n_flat - 1)

    def gather_copy(j, c, slot):
        return pltpu.make_async_remote_copy(
            src_ref=gath.at[c, slot], dst_ref=gath.at[c, slot],
            send_sem=s1.at[c, j], recv_sem=r1.at[c, j],
            device_id={"kcol": lax.rem(kcol + j, n_cols)}, device_id_type=MESH,
        )

    def stat_copy(j, slot):
        return pltpu.make_async_remote_copy(
            src_ref=stat1.at[slot], dst_ref=stat1.at[slot],
            send_sem=s1s.at[j], recv_sem=r1s.at[j],
            device_id={"kcol": lax.rem(kcol + j, n_cols)}, device_id_type=MESH,
        )

    @pl.loop(1, n_cols)
    def _(j):
        stat_copy(j, kcol).start()

    for c in range(chunks):

        @pl.loop(1, n_cols)
        def _(j):
            gather_copy(j, c, kcol).start()

    def exchange_copy(i, c):
        return pltpu.make_async_remote_copy(
            src_ref=blk.at[c, 0], dst_ref=blk.at[c, i],
            send_sem=s2.at[c, i], recv_sem=r2.at[c, i],
            device_id={"qrow": lax.rem(qrow + i, n_rows)}, device_id_type=MESH,
        )

    def exchange_stat(i):
        return pltpu.make_async_remote_copy(
            src_ref=stat.at[0], dst_ref=stat.at[i],
            send_sem=s2s.at[i], recv_sem=r2s.at[i],
            device_id={"qrow": lax.rem(qrow + i, n_rows)}, device_id_type=MESH,
        )

    def term_copy(i, c):
        return pltpu.make_async_remote_copy(
            src_ref=dqs.at[c, i], dst_ref=dqr.at[c, i],
            send_sem=sa.at[c, i], recv_sem=ra.at[c, i],
            device_id={"qrow": lax.rem(qrow - i + n_rows, n_rows)}, device_id_type=MESH,
        )

    def last_copy(j, c):
        z = lax.rem(kcol + j, n_cols)
        return pltpu.make_async_remote_copy(
            src_ref=dqz.at[c, 0, z], dst_ref=dqz.at[c, 1, j],
            send_sem=sb.at[c, j], recv_sem=rb.at[c, j], device_id={"kcol": z}, device_id_type=MESH,
        )

    k_pos = (kcol * n_rows + qrow) * ks + lax.broadcasted_iota(jnp.int32, (rows, ks), 1)

    def columns_of(i):
        cols_s[i] = jnp.concatenate(
            [stat[i], jnp.zeros((128 - 2 * heads, lanes), F32)], axis=0
        ).T[0:rows, :]
        group = lax.rem(qrow - i + n_rows, n_rows)
        q_pos = offset + rows * group + lax.broadcasted_iota(jnp.int32, (rows, ks), 0)
        start = jnp.full((rows, ks), offset, jnp.int32)
        begin = offset
        for d in range(spans_ref.shape[0]):
            start = jnp.where(begin <= q_pos, begin, start)
            begin = begin + spans_ref[d]
        mask = (k_pos <= q_pos) & ((k_pos >= start) | (k_pos < offset))
        mask_s[i] = jnp.where(mask, 1.0, 0.0)

    def tile(i, c, own):
        mask = mask_s[i] > 0.5
        at = pl.ds(pl.multiple_of(i * rows, 16), rows)
        for e in range(hc):
            h = c * hc + e
            cols = slice(h * depth, (h + 1) * depth)
            q = blk[c, i, e * rows : (e + 1) * rows, :]
            g = blk[c, i, (hc + e) * rows : (hc + e + 1) * rows, :]
            k = k_ref[:, cols]
            v = v_ref[:, cols]
            mult = mult_ref[h]
            nt = (((1,), (1,)), ((), ()))
            raw = lax.dot_general(q, k, nt, preferred_element_type=F32) * factor
            dprob = lax.dot_general(g, v, nt, preferred_element_type=F32)
            prob = jnp.where(mask, jnp.exp(mult * raw - cols_s[i, :, h : h + 1]), 0.0)
            ds = prob * (dprob - cols_s[i, :, heads + h : heads + h + 1])
            tau_acc[h] += jnp.sum((ds * raw).reshape(rows // 8, 8, ks), axis=0)
            gb = ((mult * factor) * ds).astype(BF16)
            prob_s[h, at, :] = prob.astype(BF16)
            grad_s[h, at, :] = gb
            term = jnp.dot(gb, k, preferred_element_type=F32)
            if own:
                dq0[c, e * rows : (e + 1) * rows, :] = term
            else:
                dqs[c, i, e * rows : (e + 1) * rows, :] = term.astype(BF16)

    for c in range(chunks):

        @pl.loop(1, n_cols)
        def _(j):
            gather_copy(j, c, lax.rem(kcol - j + n_cols, n_cols)).wait_recv()

        for z in range(n_cols):
            pack32[...] = gath[c, z].astype(F32)
            for e in range(2 * hc):
                asm32[e * rows + z * qs : e * rows + (z + 1) * qs, :] = pack32[e * qs : (e + 1) * qs, :]
        blk[c, 0] = asm32[0 : 2 * hc * rows, :].astype(BF16)

        if c == 0:

            @pl.loop(1, n_cols)
            def _(j):
                stat_copy(j, lax.rem(kcol - j + n_cols, n_cols)).wait_recv()

            total = stat1[0]
            for z in range(1, n_cols):
                total = total + stat1[z]
            stat[0] = total

            @pl.loop(1, n_rows)
            def _(i):
                exchange_stat(i).start()

        @pl.loop(1, n_rows)
        def _(i):
            exchange_copy(i, c).start()

        if c == 0:
            load_k.wait()
            load_v.wait()
            columns_of(0)
        tile(0, c, True)

    pad = dqz.shape[3]

    def settle(c):
        @pl.loop(1, n_rows)
        def _(i):
            term_copy(i, c).wait_recv()
            dq0[c] += dqr[c, i].astype(F32)

        for z in range(n_cols):
            for e in range(hc):
                pack32[e * qs : (e + 1) * qs, :] = dq0[
                    c, e * rows + z * qs : e * rows + (z + 1) * qs, :
                ]
            dqz[c, 0, z] = pack32[0:pad, :].astype(BF16)

        @pl.loop(1, n_cols)
        def _(j):
            last_copy(j, c).start()

    for c in range(chunks):

        @pl.loop(1, n_rows)
        def _(i):
            if c == 0:
                exchange_stat(i).wait_recv()
                columns_of(i)
            exchange_copy(i, c).wait_recv()
            tile(i, c, False)
            term_copy(i, c).start()

        if c >= 1:
            settle(c - 1)

    tau_a[flat] = jnp.sum(tau_acc[...], axis=1)

    def tau_copy(t, slot):
        peer = lax.rem(flat + t, n_flat)
        return pltpu.make_async_remote_copy(
            src_ref=tau_a.at[slot], dst_ref=tau_a.at[slot],
            send_sem=sta.at[t], recv_sem=rta.at[t],
            device_id={"qrow": lax.rem(peer, n_rows), "dp": peer // n_rows}, device_id_type=MESH,
        )

    @pl.loop(1, n_flat)
    def _(t):
        tau_copy(t, flat).start()

    tn = (((0,), (0,)), ((), ()))
    for h in range(heads):
        c, e = h // hc, h % hc
        cols = slice(h * depth, (h + 1) * depth)
        q_all = blk[c, :, e * rows : (e + 1) * rows, :].reshape(n_rows * rows, depth)
        g_all = blk[c, :, (hc + e) * rows : (hc + e + 1) * rows, :].reshape(n_rows * rows, depth)
        dk_ref[:, cols] = lax.dot_general(
            grad_s[h], q_all, tn, preferred_element_type=F32
        ).astype(BF16)
        dv_ref[:, cols] = lax.dot_general(
            prob_s[h], g_all, tn, preferred_element_type=F32
        ).astype(BF16)
    store_k = pltpu.make_async_copy(dk_ref, dk_hbm, local_sem.at[2])
    store_v = pltpu.make_async_copy(dv_ref, dv_hbm, local_sem.at[3])
    store_k.start()
    store_v.start()

    settle(chunks - 1)

    @pl.loop(1, n_flat)
    def _(t):
        tau_copy(t, lax.rem(flat - t + n_flat, n_flat)).wait_recv()

    tau_b[kcol] = jnp.sum(
        tau_a[...].reshape(n_dp, n_rows, heads, 128), axis=1
    ).reshape(n_dp * heads, 128)

    def last_tau(j, slot):
        return pltpu.make_async_remote_copy(
            src_ref=tau_b.at[slot], dst_ref=tau_b.at[slot],
            send_sem=stb.at[j], recv_sem=rtb.at[j],
            device_id={"kcol": lax.rem(kcol + j, n_cols)}, device_id_type=MESH,
        )

    @pl.loop(1, n_cols)
    def _(j):
        last_tau(j, kcol).start()

    for c in range(chunks):
        pack32[0:pad, :] = dqz[c, 0, kcol].astype(F32)

        @pl.loop(1, n_cols)
        def _(j):
            last_copy(j, c).wait_recv()
            pack32[0:pad, :] += dqz[c, 1, j].astype(F32)

        for e in range(hc):
            h = c * hc + e
            dq_ref[:, h * depth : (h + 1) * depth] = pack32[e * qs : (e + 1) * qs, :].astype(BF16)

    @pl.loop(1, n_cols)
    def _(j):
        last_tau(j, lax.rem(kcol - j + n_cols, n_cols)).wait_recv()

    tau = jnp.sum(tau_b[...], axis=0)
    tau = jnp.concatenate([tau, jnp.zeros((128 - n_dp * heads, 128), F32)], axis=0).T
    tau_ref[...] = jnp.sum(tau, axis=0, keepdims=True)[:, 0 : n_dp * heads]

    @pl.loop(1, n_cols)
    def _(j):
        stat_copy(j, kcol).wait_send()
        last_tau(j, kcol).wait_send()
        for c in range(chunks):
            gather_copy(j, c, kcol).wait_send()
            last_copy(j, c).wait_send()

    @pl.loop(1, n_rows)
    def _(i):
        exchange_stat(i).wait_send()
        for c in range(chunks):
            exchange_copy(i, c).wait_send()
            term_copy(i, c).wait_send()

    @pl.loop(1, n_flat)
    def _(t):
        tau_copy(t, flat).wait_send()

    store_k.wait()
    store_v.wait()


def hand_on(dq_in, dk_in, dv_in, tau_in, dq_out, dk_out, dv_out, tau_out):
    dq_out[...] = dq_in[...]
    dk_out[...] = dk_in[...]
    dv_out[...] = dv_in[...]
    tau_out[...] = tau_in[...]


def local(q, k, v, o, g, lse, mult, spans):
    heads = mult.shape[0]
    qs, width = q.shape
    ks = k.shape[0]
    depth = width // heads
    n_rows = lax.axis_size("qrow")
    n_cols = lax.axis_size("kcol")
    n_dp = lax.axis_size("dp")
    rows = n_cols * qs
    lanes = -(-rows // 128) * 128
    chunks = CHUNKS
    hc = heads // chunks
    pad = -(-hc * qs // 16) * 16
    dims = (n_rows, n_cols, n_dp, heads, depth, qs, ks, lanes, chunks)
    n_flat = n_rows * n_dp
    vmem = pl.BlockSpec(memory_space=pltpu.VMEM)
    smem = pl.BlockSpec(memory_space=pltpu.SMEM)
    hbm = pl.BlockSpec(memory_space=pl.ANY)
    dma = pltpu.SemaphoreType.DMA
    macs = 5 * heads * n_rows * rows * ks * depth
    shapes = (
        jax.ShapeDtypeStruct((qs, width), BF16),
        jax.ShapeDtypeStruct((ks, width), BF16),
        jax.ShapeDtypeStruct((ks, width), BF16),
        jax.ShapeDtypeStruct((1, n_dp * heads), F32),
    )
    results = pl.pallas_call(
        functools.partial(kernel, dims),
        out_shape=shapes,
        in_specs=[vmem, hbm, hbm, vmem, vmem, vmem, smem, smem],
        out_specs=(vmem, hbm, hbm, vmem),
        scratch_shapes=[
            pltpu.VMEM((ks, width), BF16),
            pltpu.VMEM((ks, width), BF16),
            pltpu.VMEM((ks, width), BF16),
            pltpu.VMEM((ks, width), BF16),
            pltpu.VMEM((2 * hc * qs, depth), F32),
            pltpu.VMEM((max(128, 2 * hc * rows), depth), F32),
            pltpu.VMEM((chunks, n_cols, 2 * hc * qs, depth), BF16),
            pltpu.VMEM((n_cols, 2 * heads, lanes), F32),
            pltpu.VMEM((chunks, n_rows, 2 * hc * rows, depth), BF16),
            pltpu.VMEM((n_rows, 2 * heads, lanes), F32),
            pltpu.VMEM((n_rows, rows, 128), F32),
            pltpu.VMEM((n_rows, rows, ks), F32),
            pltpu.VMEM((heads, n_rows * rows, ks), BF16),
            pltpu.VMEM((heads, n_rows * rows, ks), BF16),
            pltpu.VMEM((chunks, n_rows, hc * rows, depth), BF16),
            pltpu.VMEM((chunks, n_rows, hc * rows, depth), BF16),
            pltpu.VMEM((chunks, hc * rows, depth), F32),
            pltpu.VMEM((chunks, 2, n_cols, pad, depth), BF16),
            pltpu.VMEM((heads, 8, ks), F32),
            pltpu.VMEM((n_flat, heads, 128), F32),
            pltpu.VMEM((n_cols, n_dp * heads, 128), F32),
            dma((4,)),
            dma((chunks, n_cols)), dma((chunks, n_cols)), dma((n_cols,)), dma((n_cols,)),
            dma((chunks, n_rows)), dma((chunks, n_rows)), dma((n_rows,)), dma((n_rows,)),
            dma((chunks, n_rows)), dma((chunks, n_rows)), dma((chunks, n_cols)), dma((chunks, n_cols)),
            dma((n_flat,)), dma((n_flat,)), dma((n_cols,)), dma((n_cols,)),
        ],
        compiler_params=pltpu.CompilerParams(
            collective_id=0, has_side_effects=True, vmem_limit_bytes=58 * 1024 * 1024
        ),
        cost_estimate=pl.CostEstimate(
            flops=2 * macs, bytes_accessed=8 * ks * width, transcendentals=heads * n_rows * rows * ks
        ),
    )(q, k, v, o, g, lse, mult, spans)
    dq, dk, dv, tau = pl.pallas_call(
        hand_on,
        out_shape=shapes,
        in_specs=[vmem] * 4,
        out_specs=(vmem,) * 4,
    )(*results)
    return dq, dk, dv, tau.reshape(-1)


def solution(mesh):
    in_specs = (
        P(("qrow", "kcol"), "dp"),
        P(("kcol", "qrow"), "dp"),
        P(("kcol", "qrow"), "dp"),
        P(("qrow", "kcol"), "dp"),
        P(("qrow", "kcol"), "dp"),
        P("dp", ("qrow", "kcol")),
        P("dp"),
        P(),
    )
    out_specs = (
        P(("qrow", "kcol"), "dp"),
        P(("kcol", "qrow"), "dp"),
        P(("kcol", "qrow"), "dp"),
        P(),
    )
    return jax.shard_map(local, mesh=mesh, in_specs=in_specs, out_specs=out_specs, check_vma=False)
```

time: 42 us -> 36.3 us (0.86)
  local copies, waits for them, and re-layouts: 4.31 us -> 0 us
  Pallas kernels: 36.8 us -> 35.5 us
    unnamed x8 -> x0, local copies, waits for them, and re-layouts: 4.31 us -> none
    pallas_call x1 -> x2, Pallas kernels: 36.8 us -> 35.5 us  [the longest x1 33.6 us: local(): pl.pallas_call(functools.partial(kernel, dims), out_shape=shapes, in_spec...]
where the time goes in v2:
time: 36.3 us; the launch traced here: 36.1 us
  Pallas kernels  35.5 us (98%)
  between operations  0.64 us (2%)
    pallas_call x1, Pallas kernels, local(): pl.pallas_call(functools.partial(kernel, dims), out_shape=shapes, in_spec...  33.6 us
    pallas_call x1, Pallas kernels, local(): pl.pallas_call(hand_on, out_shape=shapes, in_specs=[vmem] * 4, out_specs=...  1.87 us

profile of v2, /device:TPU:0, one launch (start us, length us, event | category | flops | bytes accessed | tf_op | source)
XLA Modules:
  0.0 36.1 jit_solution(18326844413067855288)
XLA Ops:
  0.6 33.6 %shard_map.111 = (bf16[12,1024]{1,0:T(8,128)(2,1)}, bf16[128,1024]{1,0:T(8,128)(2,1)}, bf16[128,1024]{1,0:T(8,128)(2,1)}, f32[1,16]{1,0:T(1,128)}) custom-call(bf16[12,1024]{1,0:T(8,128)(2,1)} %q_ref.1, bf16[128,1024]{1,0:T(8,128)(2,1)} %k_hbm.1, bf16[128,1024]{1,0:T(8,128)(2,1)} %v_hbm.1, bf16[12,1024]{1,0:T(8,128)(2,1)} %o_ref.1, bf16[12,1024]{1,0:T(8,128)(2,1)} %g_ref.1, ...), custom_call_target="tpu_custom_call" | custom-call | flops 251658240 | bytes 1048576 | tf_op jit(solution)/shard_map/pallas_call | solution.py:382
  34.3 1.9 %shard_map.112 = (bf16[12,1024]{1,0:T(8,128)(2,1)}, bf16[128,1024]{1,0:T(8,128)(2,1)}, bf16[128,1024]{1,0:T(8,128)(2,1)}, f32[1,16]{1,0:T(1,128)}) custom-call(bf16[12,1024]{1,0:T(8,128)(2,1)} %get-tuple-element.12.dq_in, bf16[128,1024]{1,0:T(8,128)(2,1)} %get-tuple-element.13.dk_in, bf16[128,1024]{1,0:T(8,128)(2,1)} %get-tuple-element.14.dv_in, ...), custom_call_target="tpu_custom_call" | custom-call | tf_op jit(solution)/shard_map/pallas_call | solution.py:422

commit v3 on v2

--- a/solution.py
+++ b/solution.py
@@ -101,15 +101,13 @@
             device_id={"kcol": lax.rem(kcol + j, n_cols)}, device_id_type=MESH,
         )
 
-    @pl.loop(1, n_cols)
-    def _(j):
-        stat_copy(j, kcol).start()
-
     for c in range(chunks):
 
         @pl.loop(1, n_cols)
         def _(j):
             gather_copy(j, c, kcol).start()
+            if c == 0:
+                stat_copy(j, kcol).start()
 
     def exchange_copy(i, c):
         return pltpu.make_async_remote_copy(
@@ -193,6 +191,10 @@
                 asm32[e * rows + z * qs : e * rows + (z + 1) * qs, :] = pack32[e * qs : (e + 1) * qs, :]
         blk[c, 0] = asm32[0 : 2 * hc * rows, :].astype(BF16)
 
+        @pl.loop(1, n_rows)
+        def _(i):
+            exchange_copy(i, c).start()
+
         if c == 0:
 
             @pl.loop(1, n_cols)
@@ -208,16 +210,12 @@
             def _(i):
                 exchange_stat(i).start()
 
-        @pl.loop(1, n_rows)
-        def _(i):
-            exchange_copy(i, c).start()
-
-        if c == 0:
-            load_k.wait()
-            load_v.wait()
-            columns_of(0)
+
+    load_k.wait()
+    load_v.wait()
+    columns_of(0)
+    for c in range(chunks):
         tile(0, c, True)
-
     pad = dqz.shape[3]
 
     def settle(c):
@@ -422,8 +420,19 @@
     dq, dk, dv, tau = pl.pallas_call(
         hand_on,
         out_shape=shapes,
-        in_specs=[vmem] * 4,
-        out_specs=(vmem,) * 4,
+        grid=(2,),
+        in_specs=[
+            pl.BlockSpec((qs, width // 2), lambda n: (0, n)),
+            pl.BlockSpec((ks // 2, width), lambda n: (n, 0)),
+            pl.BlockSpec((ks // 2, width), lambda n: (n, 0)),
+            pl.BlockSpec((1, n_dp * heads), lambda n: (0, 0)),
+        ],
+        out_specs=(
+            pl.BlockSpec((qs, width // 2), lambda n: (0, n)),
+            pl.BlockSpec((ks // 2, width), lambda n: (n, 0)),
+            pl.BlockSpec((ks // 2, width), lambda n: (n, 0)),
+            pl.BlockSpec((1, n_dp * heads), lambda n: (0, 0)),
+        ),
     )(*results)
     return dq, dk, dv, tau.reshape(-1)
 

time: 36.3 us -> 36 us (level)
  no operation moved by 1% of the time
where the time goes in v3:
time: 36 us; the launch traced here: 35.8 us
  Pallas kernels  35.2 us (98%)
  between operations  0.64 us (2%)
    pallas_call x1, Pallas kernels, local(): pl.pallas_call(functools.partial(kernel, dims), out_shape=shapes, in_spec...  33.3 us
    pallas_call x1, Pallas kernels, local(): pl.pallas_call(hand_on, out_shape=shapes, grid=(2,), in_specs=[pl.BlockSp...  1.88 us

profile of v3, /device:TPU:0, one launch (start us, length us, event | category | flops | bytes accessed | tf_op | source)
XLA Modules:
  0.0 35.8 jit_solution(9514579555266300823)
XLA Ops:
  0.6 33.3 %shard_map.111 = (bf16[12,1024]{1,0:T(8,128)(2,1)}, bf16[128,1024]{1,0:T(8,128)(2,1)}, bf16[128,1024]{1,0:T(8,128)(2,1)}, f32[1,16]{1,0:T(1,128)}) custom-call(bf16[12,1024]{1,0:T(8,128)(2,1)} %q_ref.1, bf16[128,1024]{1,0:T(8,128)(2,1)} %k_hbm.1, bf16[128,1024]{1,0:T(8,128)(2,1)} %v_hbm.1, bf16[12,1024]{1,0:T(8,128)(2,1)} %o_ref.1, bf16[12,1024]{1,0:T(8,128)(2,1)} %g_ref.1, ...), custom_call_target="tpu_custom_call" | custom-call | flops 251658240 | bytes 1048576 | tf_op jit(solution)/shard_map/pallas_call | solution.py:380
  33.9 1.9 %shard_map.112 = (bf16[12,1024]{1,0:T(8,128)(2,1)}, bf16[128,1024]{1,0:T(8,128)(2,1)}, bf16[128,1024]{1,0:T(8,128)(2,1)}, f32[1,16]{1,0:T(1,128)}) custom-call(bf16[12,1024]{1,0:T(8,128)(2,1)} %get-tuple-element.12.dq_in, bf16[128,1024]{1,0:T(8,128)(2,1)} %get-tuple-element.13.dk_in, bf16[128,1024]{1,0:T(8,128)(2,1)} %get-tuple-element.14.dv_in, ...), custom_call_target="tpu_custom_call" | custom-call | tf_op jit(solution)/shard_map/pallas_call | solution.py:420
